TPU v7x, 32 devices: a whole 2x2x4 slice. The times are simulated.
32 devices in a mesh: src: 8 (over z, y), sta: 4 (over x, core).
Axes of the slice: x: 2, y: 2, z: 4, core: 2. Of those that a mesh axis runs over, the one named last changes fastest.
Arguments:
- trace: float32 [256, 8256], P('sta', 'src'), may hold values from -6 to 6
- quadrature: float32 [256, 8256], P('sta', 'src'), may hold values from -6 to 6
- gains: float32 [256], P('sta'), may hold values from 0.3 to 3
- lags: int32 [1024, 256], P('src', 'sta'), may hold values from 0 to 63
Outputs:
- beam_power: float32 [2, 1024], P(None, 'src')
All inputs are finite; a program needn't handle non-finite values.
Results may differ from a plain program's by a relative error of at most 0.0003.
Values may be sent and summed in bfloat16 or wider, within the bound.
A program may use at most 256 MiB of HBM per device.

v0:
```python
import jax
import jax.numpy as jnp
from jax import lax
from jax.sharding import PartitionSpec as P

W = 4096
LAGS = 64
STEPS = 2


def on_device(trace, quadrature, gains, lags):
    energy = trace * trace + quadrature * quadrature
    row_totals = lax.psum(jnp.sum(energy, axis=1), "src")
    baseline = row_totals / (energy.shape[1] * lax.axis_size("src"))
    weighted = (gains[:, None] * (energy - baseline[:, None])).astype(jnp.bfloat16)
    envelope = lax.all_gather(weighted, "src", axis=1, tiled=True)
    cell_count, station_count = lags.shape
    offsets = jnp.arange(LAGS, dtype=jnp.int32)
    selector = (lags[:, None, :] == offsets[None, :, None]).astype(jnp.bfloat16)
    selector = selector.reshape(cell_count, LAGS * station_count)
    power_rows = []
    for step_index in range(STEPS):
        start = step_index * W
        stacked = jnp.concatenate(
            [envelope[:, start + lag_index : start + lag_index + W] for lag_index in range(LAGS)],
            axis=0,
        )
        partial_beam = jnp.dot(selector, stacked, preferred_element_type=jnp.float32)
        beam_share = lax.psum_scatter(partial_beam, "sta", scatter_dimension=1, tiled=True)
        power_rows.append(lax.psum(jnp.sum(beam_share * beam_share, axis=1), "sta"))
    power = jnp.stack(power_rows)
    peak_power = lax.pmax(jnp.max(power, axis=1), "src")
    return power / peak_power[:, None]


def solution(mesh):
    return jax.shard_map(
        on_device,
        mesh=mesh,
        in_specs=(P("sta", "src"), P("sta", "src"), P("sta"), P("src", "sta")),
        out_specs=P(None, "src"),
        check_vma=False,
    )
```

profile of v0, /device:TPU:0, one launch (start us, length us, event | category | flops | bytes accessed | tf_op | source)
XLA Modules:
  0.0 275.1 jit_solution(4937442570417108137)
XLA Ops:
  6.5 1.2 fusion.1
  7.7 23.1 %psum.21 = f32[64]{0:T(128)S(1)} all-reduce(f32[64]{0:T(128)S(1)} %fusion.1), channel_id=1, replica_groups=mesh['src'=8,'sta'=4] {'src'}, use_global_device_ids=true, to_apply=%region_1.0 | all-reduce | flops 64 | bytes 512 | tf_op jit(solution)/shard_map/psum | solution.py:13
  30.9 1.8 fusion
  32.8 1.5 bitcast_compare_fusion
  34.3 36.9 %all-gather.3.cloned.1.call-done = bf16[8,1032,64]{1,2,0:T(8,128)(2,1)} async-done(((bf16[1,1032,64]{1,2,0:T(8,128)(2,1)}), bf16[8,1032,64]{1,2,0:T(8,128)(2,1)}) %all-gather.3.cloned.1.call-update) | async-done | bytes 1056784 | tf_op jit(solution)/shard_map/all_gather | solution.py:16
  71.2 1.9 copy.7
  75.0 1.2 slice_dynamic-update-slice_fusion.126
  76.2 1.2 slice_dynamic-update-slice_fusion.125
  84.4 1.2 slice_dynamic-update-slice_fusion.118
  85.6 1.2 slice_dynamic-update-slice_fusion.117
  90.3 1.2 slice_dynamic-update-slice_fusion.113
  91.5 1.2 slice_dynamic-update-slice_fusion.112
  92.7 1.2 slice_dynamic-update-slice_fusion.111
  95.1 1.2 slice_dynamic-update-slice_fusion.109
  100.9 1.2 slice_dynamic-update-slice_fusion.104
  109.2 1.2 slice_dynamic-update-slice_fusion.97
  112.7 1.4 slice_dynamic-update-slice_fusion.94
  115.2 1.2 slice_dynamic-update-slice_fusion.92
  122.3 1.2 slice_dynamic-update-slice_fusion.86
  128.1 1.2 slice_dynamic-update-slice_fusion.81
  129.3 1.2 slice_dynamic-update-slice_fusion.80
  130.5 1.2 slice_dynamic-update-slice_fusion.79
  132.9 1.2 slice_dynamic-update-slice_fusion.77
  138.7 1.2 slice_dynamic-update-slice_fusion.72
  145.8 1.2 slice_dynamic-update-slice_fusion.66
  149.3 11.1 %copy-done = bf16[4096,4096]{1,0:T(8,128)(2,1)} copy-done((bf16[4096,4096]{1,0:T(8,128)(2,1)}, bf16[4096,4096]{1,0:T(8,128)(2,1)S(1)}, u32[]{:S(2)}) %copy-start) | copy-done | bytes 33554456
  160.4 14.4 %fusion.3 = f32[128,4096]{1,0:T(8,128)} fusion(pred[128,4096]{0,1:T(32,128)(4,1)S(1)} %bitcast_compare_fusion, bf16[4096,4096]{1,0:T(8,128)(2,1)} %copy-done), kind=kOutput, calls=%fused_computation.139 | convolution fusion | flops 4294967296 | bytes 36175872 | tf_op jit(solution)/shard_map/dot_general | solution.py:28
  174.8 15.4 %fusion.4 = f32[128,4096]{1,0:T(8,128)} fusion(pred[128,4096]{0,1:T(32,128)(4,1)S(1)} %bitcast_compare_fusion, bf16[4096,4096]{1,0:T(8,128)(2,1)} %get-tuple-element.8), kind=kOutput, calls=%fused_computation.140 | convolution fusion | flops 4294967296 | bytes 36175872 | tf_op jit(solution)/shard_map/dot_general | solution.py:28
  190.3 14.8 %reduce-scatter.3.cloned.1.call-done = f32[128,1024]{1,0:T(8,128)} async-done(((f32[128,4096]{1,0:T(8,128)}), f32[128,1024]{1,0:T(8,128)}) %reduce-scatter.3.cloned.1.call-update) | async-done | bytes 524304 | tf_op jit(solution)/shard_map/reduce_scatter | solution.py:29
  206.3 33.0 %reduce-scatter.5.cloned.1.call-done = f32[128,1024]{1,0:T(8,128)} async-done(((f32[128,4096]{1,0:T(8,128)}), f32[128,1024]{1,0:T(8,128)}) %reduce-scatter.5.cloned.1.call-update) | async-done | bytes 524304 | tf_op jit(solution)/shard_map/reduce_scatter | solution.py:29
  240.4 5.8 %all-reduce = (f32[1,128]{1,0:T(1,128)S(1)}, f32[1,128]{1,0:T(1,128)S(1)}) all-reduce(f32[1,128]{1,0:T(1,128)S(1)} %bitcast.80, f32[1,128]{1,0:T(1,128)S(1)} %bitcast.79), channel_id=1, replica_groups=mesh['src'=8,'sta'=4] {'sta'}, use_global_device_ids=true, to_apply=%region_7.0 | all-reduce | flops 256 | bytes 2048 | tf_op jit(solution)/shard_map/psum | solution.py:30
  246.3 21.6 %pmax.7 = f32[2]{0:T(128)S(1)} all-reduce(f32[2]{0:T(128)S(1)} %fusion.2), channel_id=1, replica_groups=mesh['src'=8,'sta'=4] {'src'}, use_global_device_ids=true, to_apply=%region_9.0 | all-reduce | flops 2 | bytes 16 | tf_op jit(solution)/shard_map/pmax | solution.py:32
  (60 shorter events, 56.6 us)
Async XLA Ops:
  6.5 64.6 %all-gather.3.cloned.1.call-start = ((), (), s32[]{:S(2)}) async-start(), calls=%async_computation.4 | async-start | bytes 1327104 | tf_op jit(solution)/shard_map/all_gather | solution.py:16
  32.7 172.4 %reduce-scatter.3.cloned.1.call-start = ((), (), s32[]{:S(2)}) async-start(), calls=%async_computation.2 | async-start | bytes 2621440 | tf_op jit(solution)/shard_map/reduce_scatter | solution.py:29
  149.3 11.1 %copy-start = (bf16[4096,4096]{1,0:T(8,128)(2,1)}, bf16[4096,4096]{1,0:T(8,128)(2,1)S(1)}, u32[]{:S(2)}) copy-start(bf16[4096,4096]{1,0:T(8,128)(2,1)S(1)} %get-tuple-element.7) | copy-start | bytes 100663296
  174.8 64.5 %reduce-scatter.5.cloned.1.call-start = ((), (), s32[]{:S(2)}) async-start(), calls=%async_computation.3 | async-start | bytes 2621440 | tf_op jit(solution)/shard_map/reduce_scatter | solution.py:29
Sparse Core Ops, SparseCore 0:
  32.8 38.3 all-gather.2
  174.9 30.1 reduce-scatter.2
  207.8 31.4 reduce-scatter.4
where the time goes:
time: 275 us
  local copies, waits for them, and re-layouts  89.2 us (32%)
  waiting for transfers between devices  84.7 us (31%)
  blocking collectives  50.5 us (18%)
  matrix products  29.8 us (11%)
  between operations  13.2 us (5%)
  other arithmetic  7.57 us (3%)
    unnamed x66, local copies, waits for them, and re-layouts  86.1 us
    reduce_scatter x2, waiting for transfers between devices, on_device(): lax.psum_scatter(partial_beam, 'sta', scatter_dimension=1, tiled=True)  47.8 us
    all_gather x1, waiting for transfers between devices, on_device(): envelope = lax.all_gather(weighted, 'src', axis=1, tiled=True)  36.9 us
    dot_general x2, matrix products, on_device(): jnp.dot(selector, stacked, preferred_element_type=jnp.float32)  29.8 us
    psum x1, blocking collectives, on_device(): row_totals = lax.psum(jnp.sum(energy, axis=1), 'src')  23.1 us
    pmax x1, blocking collectives, on_device(): peak_power = lax.pmax(jnp.max(power, axis=1), 'src')  21.6 us
    psum x1, blocking collectives, on_device(): power_rows.append(lax.psum(jnp.sum(beam_share * beam_share, axis=1), 'sta'))  5.76 us
  transfers between devices with their start and end apart: 3, of which 3 were waited for; matrix products, arithmetic and copies ran while one was open for 7% of the time, Pallas kernels for 0%

commit v1 on v0

v1 whole, which is shorter than its diff:
```python
import functools

import jax
import jax.numpy as jnp
from jax import lax
from jax.experimental import pallas as pl
from jax.experimental.pallas import tpu as pltpu
from jax.sharding import PartitionSpec as P

W = 4096
LAGS = 64
STEPS = 2
SUB = 16
CORES = 2


def kernel(
    n_src, n_sta,
    trace_ref, quad_ref, gains_ref, lags_ref, out_ref,
    energy_t, edge_out, edge_in, stat, lag_all, lag_group, packed, wide, shifted, picks, acc, part, whole,
    stat_send, stat_recv, edge_send, edge_recv, lag_send, lag_recv, group_send, group_recv,
    pack_send, pack_recv, fwd_send, fwd_recv, part_send, part_recv, whole_send, whole_recv,
):
    i = lax.axis_index("src")
    j = lax.axis_index("sta")
    stations, block = trace_ref.shape
    cells = lags_ref.shape[0]
    span = STEPS * W // n_src
    rows = span + LAGS
    half = rows // 2
    per = n_src // n_sta
    chips = n_sta // CORES
    chip, core = j // CORES, j % CORES
    mate = chip * CORES + (1 - core)

    def remote(src, dst, send, recv, where):
        copy = pltpu.make_async_remote_copy(
            src_ref=src, dst_ref=dst, send_sem=send, recv_sem=recv,
            device_id=where, device_id_type=pl.DeviceIdType.MESH,
        )
        copy.start()
        return copy

    def src_at(d):
        return ((i + d) % n_src, j)

    def sta_at(d):
        return (i, (j + d) % n_sta)

    barrier = pltpu.get_barrier_semaphore()
    for d in range(1, n_src):
        pl.semaphore_signal(barrier, inc=1, device_id=src_at(d), device_id_type=pl.DeviceIdType.MESH)
    for d in range(1, n_sta):
        pl.semaphore_signal(barrier, inc=1, device_id=sta_at(d), device_id_type=pl.DeviceIdType.MESH)

    own = trace_ref[...] * trace_ref[...] + quad_ref[...] * quad_ref[...]
    own_t = own.T
    energy_t[LAGS : LAGS + block, :] = own_t
    edge_out[0] = own_t[:LAGS]
    edge_out[1] = own_t[block - LAGS :]
    stat[0] = jnp.sum(own_t, axis=0, keepdims=True)
    lag_all[i] = lags_ref[...].astype(jnp.float32).T.astype(jnp.bfloat16)
    pl.semaphore_wait(barrier, n_src + n_sta - 2)

    stat_copies = [remote(stat.at[0], stat.at[d], stat_send.at[d], stat_recv.at[d], src_at(d)) for d in range(1, n_src)]
    edge_copies = [
        remote(edge_out.at[0], edge_in.at[1], edge_send.at[0], edge_recv.at[1], src_at(n_src - 1)),
        remote(edge_out.at[1], edge_in.at[0], edge_send.at[1], edge_recv.at[0], src_at(1)),
    ]
    lag_copies = [remote(lag_all.at[i], lag_all.at[i], lag_send.at[d], lag_recv.at[d], src_at(d)) for d in range(1, n_src)]

    for copy in stat_copies + edge_copies:
        copy.wait_recv()
    baseline = jnp.sum(stat[...], axis=0) / (block * n_src)
    energy_t[0:LAGS, :] = edge_in[0]
    energy_t[LAGS + block :, :] = edge_in[1]
    offset = LAGS - (LAGS // n_src) * i
    upper = gains_ref[...] * (energy_t[pl.ds(offset, half), :] - baseline)
    lower = gains_ref[...] * (energy_t[pl.ds(offset + half, half), :] - baseline)
    packed[j] = jnp.concatenate([upper, lower], axis=1).astype(jnp.bfloat16)

    pack_copies = [remote(packed.at[j], packed.at[j], pack_send.at[0], pack_recv.at[0], (i, mate))]
    for c in range(1, chips):
        there = (j + c * CORES) % n_sta
        pack_copies.append(remote(packed.at[j], packed.at[j], pack_send.at[c], pack_recv.at[c], (i, there)))

    for copy in lag_copies:
        copy.wait_recv()
    group_copies = []
    for d in range(1, n_sta):
        there = (j + d) % n_sta
        group_copies.append(remote(
            lag_all.at[pl.ds(there * per, per)], lag_group.at[j], group_send.at[d], group_recv.at[d], (i, there),
        ))
    lag_group[j] = lag_all[pl.ds(j * per, per)]

    pack_copies[0].wait_recv()
    for copy in group_copies:
        copy.wait_recv()

    low_lanes = lax.broadcasted_iota(jnp.int32, (half, 2 * stations), 1) < stations
    acc[...] = jnp.zeros_like(acc)
    copied = span + LAGS - SUB
    for phase in range(chips):
        first = ((chip + phase) % chips) * CORES
        if phase >= 1:
            source = (j + (chips - phase) * CORES) % n_sta
            fwd_copies[phase - 1].wait_recv()
        a = packed[first].astype(jnp.float32)
        b = packed[first + 1].astype(jnp.float32)
        wide[0:half, :] = jnp.where(low_lanes, a, pltpu.roll(b, stations, 1))
        wide[half:rows, :] = jnp.where(low_lanes, pltpu.roll(a, stations, 1), b)
        for s in range(SUB):
            shifted[s] = wide[s : s + copied, :].astype(jnp.bfloat16)
        lag_pair = jnp.concatenate(
            [jnp.concatenate([lag_group[first + c, q] for q in range(per)], axis=1) for c in range(CORES)], axis=0
        )
        if phase == 0:
            fwd_copies = []
            for c in range(1, chips):
                pack_copies[c].wait_recv()
                source = (j + (chips - c) * CORES) % n_sta
                fwd_copies.append(remote(
                    packed.at[source], packed.at[source], fwd_send.at[c], fwd_recv.at[c], (i, mate),
                ))

        def add_lags(coarse, carry):
            start = pl.multiple_of(coarse * SUB, SUB)
            for s in range(SUB):
                lag = (start + s).astype(jnp.float32).astype(jnp.bfloat16)
                picks[s * 2 * stations : (s + 1) * 2 * stations, :] = jnp.where(
                    lag_pair == lag, jnp.bfloat16(1), jnp.bfloat16(0)
                )
            left = jnp.concatenate([shifted[s, pl.ds(start, span), :] for s in range(SUB)], axis=1)
            acc[...] += jnp.dot(left, picks[...], preferred_element_type=jnp.float32)
            return carry

        lax.fori_loop(0, LAGS // SUB, add_lags, 0)

    part[i] = jnp.sum(acc[...] * acc[...], axis=0, keepdims=True)
    part_copies = [remote(part.at[i], part.at[i], part_send.at[d], part_recv.at[d], src_at(d)) for d in range(1, n_src)]
    for copy in part_copies:
        copy.wait_recv()
    share = n_src // STEPS
    whole[j] = jnp.concatenate(
        [jnp.sum(part[k * share : (k + 1) * share], axis=0) for k in range(STEPS)], axis=0
    )
    whole_copies = [remote(whole.at[j], whole.at[j], whole_send.at[d], whole_recv.at[d], sta_at(d)) for d in range(1, n_sta)]
    for copy in whole_copies:
        copy.wait_recv()
    peak = jnp.max(jnp.max(whole[...], axis=0), axis=1, keepdims=True)
    mine = whole[i // per]
    place = i % per
    result = mine[:, :cells]
    for q in range(1, per):
        result = jnp.where(place == q, mine[:, q * cells : (q + 1) * cells], result)
    out_ref[...] = result / peak
    for copy in stat_copies + edge_copies + lag_copies + pack_copies + group_copies + fwd_copies + part_copies + whole_copies:
        copy.wait_send()


def on_device(n_src, n_sta, trace, quadrature, gains, lags):
    stations, block = trace.shape
    cells = lags.shape[0]
    per = n_src // n_sta
    chips = n_sta // CORES
    span = STEPS * W // n_src
    rows = span + LAGS
    dma = pltpu.SemaphoreType.DMA
    return pl.pallas_call(
        functools.partial(kernel, n_src, n_sta),
        out_shape=jax.ShapeDtypeStruct((STEPS, cells), jnp.float32),
        in_specs=[pl.BlockSpec(memory_space=pltpu.VMEM)] * 4,
        out_specs=pl.BlockSpec(memory_space=pltpu.VMEM),
        scratch_shapes=[
            pltpu.VMEM((block + 2 * LAGS, stations), jnp.float32),
            pltpu.VMEM((2, LAGS, stations), jnp.float32),
            pltpu.VMEM((2, LAGS, stations), jnp.float32),
            pltpu.VMEM((n_src, 1, stations), jnp.float32),
            pltpu.VMEM((n_src, stations, cells), jnp.bfloat16),
            pltpu.VMEM((n_sta, per, stations, cells), jnp.bfloat16),
            pltpu.VMEM((n_sta, rows // 2, 2 * stations), jnp.bfloat16),
            pltpu.VMEM((rows, 2 * stations), jnp.float32),
            pltpu.VMEM((SUB, rows - SUB, 2 * stations), jnp.bfloat16),
            pltpu.VMEM((SUB * 2 * stations, per * cells), jnp.bfloat16),
            pltpu.VMEM((span, per * cells), jnp.float32),
            pltpu.VMEM((n_src, 1, per * cells), jnp.float32),
            pltpu.VMEM((n_sta, STEPS, per * cells), jnp.float32),
            dma((n_src,)), dma((n_src,)),
            dma((2,)), dma((2,)),
            dma((n_src,)), dma((n_src,)),
            dma((n_sta,)), dma((n_sta,)),
            dma((chips,)), dma((chips,)),
            dma((chips,)), dma((chips,)),
            dma((n_src,)), dma((n_src,)),
            dma((n_sta,)), dma((n_sta,)),
        ],
        compiler_params=pltpu.CompilerParams(
            collective_id=0, has_side_effects=True, vmem_limit_bytes=48 * 1024 * 1024
        ),
    )(trace, quadrature, gains.reshape(1, stations), lags)


def solution(mesh):
    return jax.shard_map(
        functools.partial(on_device, mesh.shape["src"], mesh.shape["sta"]),
        mesh=mesh,
        in_specs=(P("sta", "src"), P("sta", "src"), P("sta"), P("src", "sta")),
        out_specs=P(None, "src"),
        check_vma=False,
    )
```

time: 275 us -> 37.2 us (0.14)
  local copies, waits for them, and re-layouts: 89.2 us -> 3.35 us
  waiting for transfers between devices: 84.7 us -> 0 us
  blocking collectives: 50.5 us -> 0 us
  Pallas kernels: 0 us -> 33.6 us
  matrix products: 29.8 us -> 0 us
  between operations: 13.2 us -> 0.03 us
  other arithmetic: 7.57 us -> 0 us
    unnamed x66 -> x8, local copies, waits for them, and re-layouts: 86.1 us -> 3.35 us
    reduce_scatter x2 -> x0, waiting for transfers between devices: 47.8 us -> none  [on_device(): lax.psum_scatter(partial_beam, 'sta', scatter_dimension=1, tiled=True)]
    all_gather x1 -> x0, waiting for transfers between devices: 36.9 us -> none  [on_device(): envelope = lax.all_gather(weighted, 'src', axis=1, tiled=True)]
    pallas_call x0 -> x1, Pallas kernels: none -> 33.6 us  [on_device(): pl.pallas_call(functools.partial(kernel, n_src, n_sta), out_shape=jax.Sha...]
    dot_general x2 -> x0, matrix products: 29.8 us -> none  [on_device(): jnp.dot(selector, stacked, preferred_element_type=jnp.float32)]
    psum x2 -> x0, blocking collectives: 28.9 us -> none  [the longest x1 23.1 us: on_device(): row_totals = lax.psum(jnp.sum(energy, axis=1), 'src')]
    pmax x1 -> x0, blocking collectives: 21.6 us -> none  [on_device(): peak_power = lax.pmax(jnp.max(power, axis=1), 'src')]
    reduce_sum x3 -> x0, other arithmetic: 3.51 us -> none  [the longest x2 2.32 us: on_device(): power_rows.append(lax.psum(jnp.sum(beam_share * beam_share, axis=1), 'sta'))]
  transfers between devices with their start and end apart: 3 -> 0, of which waited for: 3 -> 0; matrix products, arithmetic and copies ran while one was open for 7% -> 0% of each run, Pallas kernels for 0% -> 0%
where the time goes in v1:
time: 37.2 us; the launch traced here: 37 us
  Pallas kernels  33.6 us (90%)
  local copies, waits for them, and re-layouts  3.35 us (9%)
    pallas_call x1, Pallas kernels, on_device(): pl.pallas_call(functools.partial(kernel, n_src, n_sta), out_shape=jax.Sha...  33.6 us
    unnamed x8, local copies, waits for them, and re-layouts  3.35 us

profile of v1, /device:TPU:0, one launch (start us, length us, event | category | flops | bytes accessed | tf_op | source)
XLA Modules:
  0.0 37.0 jit_solution(16025507093950435329)
XLA Ops:
  0.0 0.0 copy-start.2
  0.0 0.9 %copy.5.lags_ref = s32[128,64]{1,0:T(8,128)S(1)} copy(s32[128,64]{0,1:T(8,128)} %param.7) | data formatting | bytes 65536 | tf_op args[3]
  0.9 0.0 copy-done.2
  0.9 0.0 copy-start
  0.9 1.0 %copy-done = f32[64,1032]{1,0:T(8,128)S(1)} copy-done((f32[64,1032]{1,0:T(8,128)S(1)}, f32[64,1032]{1,0:T(8,128)}, u32[]{:S(2)}) %copy-start) | copy-done | bytes 264216
  1.8 0.0 copy-start.1
  1.8 1.0 %copy-done.1 = f32[64,1032]{1,0:T(8,128)S(1)} copy-done((f32[64,1032]{1,0:T(8,128)S(1)}, f32[64,1032]{1,0:T(8,128)}, u32[]{:S(2)}) %copy-start.1) | copy-done | bytes 264216
  2.8 33.6 %shard_map.46 = f32[2,128]{1,0:T(2,128)S(1)} custom-call(f32[64,1032]{1,0:T(8,128)S(1)} %copy-done, f32[64,1032]{1,0:T(8,128)S(1)} %copy-done.1, f32[1,64]{1,0:T(1,128)S(1)} %bitcast.1, s32[128,64]{1,0:T(8,128)S(1)} %copy.5.lags_ref), custom_call_target="tpu_custom_call" | custom-call | tf_op jit(solution)/shard_map/pallas_call | solution.py:170
  36.4 0.6 %copy.7 = f32[2,128]{1,0:T(2,128)} copy(f32[2,128]{1,0:T(2,128)S(1)} %shard_map.46) | data formatting | bytes 2048
Async XLA Ops:
  0.0 0.9 %copy-start.2 = (f32[64]{0:T(128)S(1)}, f32[64]{0:T(128)}, u32[]{:S(2)}) copy-start(f32[64]{0:T(128)} %param.6) | copy-start | bytes 772
  0.9 1.0 %copy-start = (f32[64,1032]{1,0:T(8,128)S(1)}, f32[64,1032]{1,0:T(8,128)}, u32[]{:S(2)}) copy-start(f32[64,1032]{1,0:T(8,128)} %trace_ref.1) | copy-start | bytes 792580
  1.8 1.0 %copy-start.1 = (f32[64,1032]{1,0:T(8,128)S(1)}, f32[64,1032]{1,0:T(8,128)}, u32[]{:S(2)}) copy-start(f32[64,1032]{1,0:T(8,128)} %quad_ref.1) | copy-start | bytes 792580

commit v2 on v1

v2 whole, which is shorter than its diff:
```python
import functools

import jax
import jax.numpy as jnp
from jax import lax
from jax.experimental import pallas as pl
from jax.experimental.pallas import tpu as pltpu
from jax.sharding import PartitionSpec as P

W = 4096
LAGS = 64
STEPS = 2
SUB = 16
CORES = 2


def kernel(
    n_src, n_sta,
    trace_hbm, quad_hbm, gains_ref, lags_hbm, out_ref,
    trace_ref, quad_ref, lags_ref, energy_t, edge_out, edge_in, total, lag_out, lag_group, packed, wide, shifted, picks, acc, part,
    load_sem, total_send, total_recv, edge_send, edge_recv, lag_send, lag_recv, pack_send, pack_recv, fwd_send, fwd_recv,
    part_send, part_recv,
):
    i = lax.axis_index("src")
    j = lax.axis_index("sta")
    stations, block = trace_ref.shape
    cells = lags_ref.shape[1]
    span = STEPS * W // n_src
    rows = span + LAGS
    half = rows // 2
    per = n_src // n_sta
    chips = n_sta // CORES
    everyone = n_src * n_sta
    chip, core = j // CORES, j % CORES
    mate = chip * CORES + (1 - core)

    def remote(src, dst, send, recv, where):
        return pltpu.make_async_remote_copy(
            src_ref=src, dst_ref=dst, send_sem=send, recv_sem=recv,
            device_id=where, device_id_type=pl.DeviceIdType.MESH,
        )

    def peer(d):
        return ((i + d // n_sta) % n_src, (j + d % n_sta) % n_sta)

    loads = [
        pltpu.make_async_copy(trace_hbm, trace_ref, load_sem.at[0]),
        pltpu.make_async_copy(quad_hbm, quad_ref, load_sem.at[1]),
        pltpu.make_async_copy(lags_hbm, lags_ref, load_sem.at[2]),
    ]
    for load in loads:
        load.start()
    barrier = pltpu.get_barrier_semaphore()

    def greet(d, carry):
        pl.semaphore_signal(barrier, inc=1, device_id=peer(d), device_id_type=pl.DeviceIdType.MESH)
        return carry

    lax.fori_loop(1, everyone, greet, 0)
    for load in loads:
        load.wait()

    lag_out[...] = lags_ref[...].astype(jnp.float32).astype(jnp.bfloat16)
    own_t = (trace_ref[...] * trace_ref[...] + quad_ref[...] * quad_ref[...]).T * gains_ref[...]
    energy_t[LAGS : LAGS + block, :] = own_t
    edge_out[0] = own_t[:LAGS]
    edge_out[1] = own_t[block - LAGS :]
    own_total = jnp.sum(own_t, axis=0, keepdims=True)
    total[i, j] = own_total
    own_mean = own_total / block
    offset = LAGS - (LAGS // n_src) * i
    upper = energy_t[pl.ds(offset, half), :] - own_mean
    lower = energy_t[pl.ds(offset + half, half), :] - own_mean
    packed[j] = jnp.concatenate([upper, lower], axis=1).astype(jnp.bfloat16)
    pl.semaphore_wait(barrier, everyone - 1)

    def total_copy(d):
        return remote(total.at[i, j], total.at[i, j], total_send.at[d], total_recv.at[d], peer(d))

    pack_copies = [remote(packed.at[j], packed.at[j], pack_send.at[0], pack_recv.at[0], (i, mate))]
    for c in range(1, chips):
        there = (j + c * CORES) % n_sta
        pack_copies.append(remote(packed.at[j], packed.at[j], pack_send.at[c], pack_recv.at[c], (i, there)))
    owner = i // per
    slot = i % per
    lag_copies = [
        remote(lag_out, lag_group.at[j, slot], lag_send.at[d], lag_recv.at[slot * n_sta + j], ((i + d) % n_src, owner))
        for d in range(n_src)
    ]
    edge_copies = []
    for d in range(n_sta):
        column = (j + d) % n_sta
        edge_copies.append(remote(
            edge_out.at[0], edge_in.at[1, j], edge_send.at[0, d], edge_recv.at[1, d], ((i + n_src - 1) % n_src, column)))
        edge_copies.append(remote(
            edge_out.at[1], edge_in.at[0, j], edge_send.at[1, d], edge_recv.at[0, d], ((i + 1) % n_src, column)))

    pack_copies[0].start()
    for copy in pack_copies[1:]:
        copy.start()
    for d in range(1, n_sta):
        total_copy(d).start()
    for copy in lag_copies[1:]:
        copy.start()

    @pl.when(owner != j)
    def _():
        lag_copies[0].start()

    @pl.when(owner == j)
    def _():
        lag_group[j, slot] = lag_out[...]

    for copy in edge_copies:
        copy.start()

    def send_total(d, carry):
        total_copy(d).start()
        return carry

    lax.fori_loop(n_sta, everyone, send_total, 0)

    for d in range(1, n_sta):
        total_copy(d).wait_recv()
    pack_copies[0].wait_recv()
    for copy in edge_copies:
        copy.wait_recv()
    for q in range(per):
        for c in range(n_sta):
            landed = remote(
                lag_out, lag_group.at[c, q], lag_send.at[0], lag_recv.at[q * n_sta + c], (i, mate))

            @pl.when(jnp.logical_or(j * per + q != i, j != c))
            def _():
                landed.wait_recv()

    low_lanes = lax.broadcasted_iota(jnp.int32, (half, 2 * stations), 1) < stations
    acc[...] = jnp.zeros_like(acc)
    copied = span + LAGS - SUB
    fwd_copies = []
    for phase in range(chips):
        first = ((chip + phase) % chips) * CORES
        if phase >= 1:
            fwd_copies[phase - 1].wait_recv()
        a = packed[first].astype(jnp.float32)
        b = packed[first + 1].astype(jnp.float32)
        wide[pl.ds(offset, half), :] = jnp.where(low_lanes, a, pltpu.roll(b, stations, 1))
        wide[pl.ds(offset + half, half), :] = jnp.where(low_lanes, pltpu.roll(a, stations, 1), b)
        for side, start in ((0, 0), (1, LAGS + block)):
            wide[start : start + LAGS, :] = jnp.concatenate(
                [edge_in[side, first + c] - total[i, first + c] / block for c in range(CORES)], axis=1
            )
        for s in range(SUB):
            shifted[s] = wide[pl.ds(offset + s, copied), :].astype(jnp.bfloat16)
        lag_pair = jnp.concatenate(
            [jnp.concatenate([lag_group[first + c, q] for q in range(per)], axis=1) for c in range(CORES)], axis=0
        )
        if phase == 0:
            for c in range(1, chips):
                pack_copies[c].wait_recv()
                source = (j + (chips - c) * CORES) % n_sta
                fwd_copies.append(remote(
                    packed.at[source], packed.at[source], fwd_send.at[c], fwd_recv.at[c], (i, mate)))
                fwd_copies[-1].start()

        def add_lags(coarse, carry):
            start = pl.multiple_of(coarse * SUB, SUB)
            for s in range(SUB):
                lag = (start + s).astype(jnp.float32).astype(jnp.bfloat16)
                picks[s * 2 * stations : (s + 1) * 2 * stations, :] = jnp.where(
                    lag_pair == lag, jnp.bfloat16(1), jnp.bfloat16(0)
                )
            left = jnp.concatenate([shifted[s, pl.ds(start, span), :] for s in range(SUB)], axis=1)
            acc[...] += jnp.dot(left, picks[...], preferred_element_type=jnp.float32)
            return carry

        lax.fori_loop(0, LAGS // SUB, add_lags, 0)

    def take_total(d, carry):
        total_copy(d).wait_recv()
        return carry

    lax.fori_loop(n_sta, everyone, take_total, 0)

    def summed(x):
        return jnp.sum(jnp.sum(jnp.sum(x, axis=0), axis=0), axis=1, keepdims=True)

    shift = summed(total[...]) / (block * n_src) - summed(total[pl.ds(i, 1)]) / block
    beam = acc[...] - shift
    part[i, j] = jnp.sum(beam * beam, axis=0, keepdims=True)

    def part_copy(d):
        return remote(part.at[i, j], part.at[i, j], part_send.at[d], part_recv.at[d], peer(d))

    def send_part(d, carry):
        part_copy(d).start()
        return carry

    def take_part(d, carry):
        part_copy(d).wait_recv()
        return carry

    lax.fori_loop(1, everyone, send_part, 0)

    for copy in edge_copies + pack_copies + fwd_copies + lag_copies[1:]:
        copy.wait_send()

    @pl.when(owner != j)
    def _():
        lag_copies[0].wait_send()

    def sent(d, carry):
        total_copy(d).wait_send()
        return carry

    lax.fori_loop(1, everyone, sent, 0)
    lax.fori_loop(1, everyone, take_part, 0)

    share = n_src // STEPS
    place = i % per
    for k in range(STEPS):
        power = jnp.sum(part[k * share : (k + 1) * share], axis=0)
        peak = jnp.max(jnp.max(power, axis=0), axis=1, keepdims=True)
        mine = jnp.sum(part[k * share : (k + 1) * share, owner], axis=0)
        result = mine[:, :cells]
        for q in range(1, per):
            result = jnp.where(place == q, mine[:, q * cells : (q + 1) * cells], result)
        out_ref[k : k + 1, :] = result / peak

    def part_sent(d, carry):
        part_copy(d).wait_send()
        return carry

    lax.fori_loop(1, everyone, part_sent, 0)


def on_device(n_src, n_sta, trace, quadrature, gains, lags):
    stations, block = trace.shape
    cells = lags.shape[0]
    per = n_src // n_sta
    chips = n_sta // CORES
    span = STEPS * W // n_src
    rows = span + LAGS
    everyone = n_src * n_sta
    dma = pltpu.SemaphoreType.DMA
    hbm = pl.BlockSpec(memory_space=pltpu.HBM)
    return pl.pallas_call(
        functools.partial(kernel, n_src, n_sta),
        out_shape=jax.ShapeDtypeStruct((STEPS, cells), jnp.float32),
        in_specs=[hbm, hbm, pl.BlockSpec(memory_space=pltpu.VMEM), hbm],
        out_specs=pl.BlockSpec(memory_space=pltpu.VMEM),
        scratch_shapes=[
            pltpu.VMEM((stations, block), jnp.float32),
            pltpu.VMEM((stations, block), jnp.float32),
            pltpu.VMEM((stations, cells), jnp.int32),
            pltpu.VMEM((block + 2 * LAGS, stations), jnp.float32),
            pltpu.VMEM((2, LAGS, stations), jnp.float32),
            pltpu.VMEM((2, n_sta, LAGS, stations), jnp.float32),
            pltpu.VMEM((n_src, n_sta, 1, stations), jnp.float32),
            pltpu.VMEM((stations, cells), jnp.bfloat16),
            pltpu.VMEM((n_sta, per, stations, cells), jnp.bfloat16),
            pltpu.VMEM((n_sta, rows // 2, 2 * stations), jnp.bfloat16),
            pltpu.VMEM((block + 2 * LAGS, 2 * stations), jnp.float32),
            pltpu.VMEM((SUB, rows - SUB, 2 * stations), jnp.bfloat16),
            pltpu.VMEM((SUB * 2 * stations, per * cells), jnp.bfloat16),
            pltpu.VMEM((span, per * cells), jnp.float32),
            pltpu.VMEM((n_src, n_sta, 1, per * cells), jnp.float32),
            dma((3,)),
            dma((everyone,)), dma((everyone,)),
            dma((2, n_sta)), dma((2, n_sta)),
            dma((n_src,)), dma((n_src,)),
            dma((chips,)), dma((chips,)),
            dma((chips,)), dma((chips,)),
            dma((everyone,)), dma((everyone,)),
        ],
        compiler_params=pltpu.CompilerParams(
            collective_id=0, has_side_effects=True, vmem_limit_bytes=48 * 1024 * 1024
        ),
    )(trace, quadrature, gains.reshape(1, stations), lags.T)


def solution(mesh):
    return jax.shard_map(
        functools.partial(on_device, mesh.shape["src"], mesh.shape["sta"]),
        mesh=mesh,
        in_specs=(P("sta", "src"), P("sta", "src"), P("sta"), P("src", "sta")),
        out_specs=P(None, "src"),
        check_vma=False,
    )
```

time: 37.2 us -> 38.8 us (1.043)
  Pallas kernels: 33.6 us -> 34.6 us
  local copies, waits for them, and re-layouts: 3.35 us -> 3.9 us
    pallas_call x1, Pallas kernels: 33.6 us -> 34.6 us  [on_device(): pl.pallas_call(functools.partial(kernel, n_src, n_sta), out_shape=jax.Sha...]
    unnamed x8 -> x9, local copies, waits for them, and re-layouts: 3.35 us -> 3.9 us
where the time goes in v2:
time: 38.8 us; the launch traced here: 38.5 us
  Pallas kernels  34.6 us (89%)
  local copies, waits for them, and re-layouts  3.9 us (10%)
    pallas_call x1, Pallas kernels, on_device(): pl.pallas_call(functools.partial(kernel, n_src, n_sta), out_shape=jax.Sha...  34.6 us
    unnamed x9, local copies, waits for them, and re-layouts  3.9 us

profile of v2, /device:TPU:0, one launch (start us, length us, event | category | flops | bytes accessed | tf_op | source)
XLA Modules:
  0.0 38.5 jit_solution(7248620522794075444)
XLA Ops:
  0.0 0.0 copy-start.3
  0.0 0.7 %copy-done.3 = f32[64]{0:T(128)S(1)} copy-done((f32[64]{0:T(128)S(1)}, f32[64]{0:T(128)}, u32[]{:S(2)}) %copy-start.3) | copy-done | bytes 280
  0.7 0.0 copy-start
  0.7 1.0 %copy-done = f32[64,1032]{1,0:T(8,128)S(1)} copy-done((f32[64,1032]{1,0:T(8,128)S(1)}, f32[64,1032]{1,0:T(8,128)}, u32[]{:S(2)}) %copy-start) | copy-done | bytes 264216
  1.6 0.0 copy-start.1
  1.6 1.0 %copy-done.1 = f32[64,1032]{1,0:T(8,128)S(1)} copy-done((f32[64,1032]{1,0:T(8,128)S(1)}, f32[64,1032]{1,0:T(8,128)}, u32[]{:S(2)}) %copy-start.1) | copy-done | bytes 264216
  2.6 0.0 copy-start.2
  2.6 0.8 %copy-done.2 = s32[128,64]{0,1:T(8,128)S(1)} copy-done((s32[128,64]{0,1:T(8,128)S(1)}, s32[128,64]{0,1:T(8,128)}, u32[]{:S(2)}) %copy-start.2) | copy-done | bytes 32792
  3.3 34.6 %shard_map.46 = f32[2,128]{1,0:T(2,128)S(1)} custom-call(f32[64,1032]{1,0:T(8,128)S(1)} %copy-done, f32[64,1032]{1,0:T(8,128)S(1)} %copy-done.1, f32[1,64]{1,0:T(1,128)S(1)} %bitcast.3, s32[64,128]{1,0:T(8,128)S(1)} %bitcast.2), custom_call_target="tpu_custom_call" | custom-call | tf_op jit(solution)/shard_map/pallas_call | solution.py:247
  38.0 0.6 %copy.6 = f32[2,128]{1,0:T(2,128)} copy(f32[2,128]{1,0:T(2,128)S(1)} %shard_map.46) | data formatting | bytes 2048
Async XLA Ops:
  0.0 0.7 %copy-start.3 = (f32[64]{0:T(128)S(1)}, f32[64]{0:T(128)}, u32[]{:S(2)}) copy-start(f32[64]{0:T(128)} %param.6) | copy-start | bytes 772
  0.7 1.0 %copy-start = (f32[64,1032]{1,0:T(8,128)S(1)}, f32[64,1032]{1,0:T(8,128)}, u32[]{:S(2)}) copy-start(f32[64,1032]{1,0:T(8,128)} %trace_hbm.1) | copy-start | bytes 792580
  1.6 1.0 %copy-start.1 = (f32[64,1032]{1,0:T(8,128)S(1)}, f32[64,1032]{1,0:T(8,128)}, u32[]{:S(2)}) copy-start(f32[64,1032]{1,0:T(8,128)} %quad_hbm.1) | copy-start | bytes 792580
  2.6 0.8 %copy-start.2 = (s32[128,64]{0,1:T(8,128)S(1)}, s32[128,64]{0,1:T(8,128)}, u32[]{:S(2)}) copy-start(s32[128,64]{0,1:T(8,128)} %param.7) | copy-start | bytes 98308

commit v3 on v2

--- a/solution.py
+++ b/solution.py
@@ -40,8 +40,15 @@
             device_id=where, device_id_type=pl.DeviceIdType.MESH,
         )
 
+    def wrap(x, n):
+        return jnp.where(x >= n, x - n, x)
+
     def peer(d):
-        return ((i + d // n_sta) % n_src, (j + d % n_sta) % n_sta)
+        return wrap(i + d // n_sta, n_src), wrap(j + d % n_sta, n_sta)
+
+    def each(low, high, step):
+        for d in range(low, high):
+            step(d, 0)
 
     loads = [
         pltpu.make_async_copy(trace_hbm, trace_ref, load_sem.at[0]),
@@ -56,7 +63,7 @@
         pl.semaphore_signal(barrier, inc=1, device_id=peer(d), device_id_type=pl.DeviceIdType.MESH)
         return carry
 
-    lax.fori_loop(1, everyone, greet, 0)
+    each(1, everyone, greet)
     for load in loads:
         load.wait()
 
@@ -79,27 +86,24 @@
 
     pack_copies = [remote(packed.at[j], packed.at[j], pack_send.at[0], pack_recv.at[0], (i, mate))]
     for c in range(1, chips):
-        there = (j + c * CORES) % n_sta
+        there = wrap(j + c * CORES, n_sta)
         pack_copies.append(remote(packed.at[j], packed.at[j], pack_send.at[c], pack_recv.at[c], (i, there)))
     owner = i // per
     slot = i % per
     lag_copies = [
-        remote(lag_out, lag_group.at[j, slot], lag_send.at[d], lag_recv.at[slot * n_sta + j], ((i + d) % n_src, owner))
+        remote(lag_out, lag_group.at[j, slot], lag_send.at[d], lag_recv.at[slot * n_sta + j], (wrap(i + d, n_src), owner))
         for d in range(n_src)
     ]
     edge_copies = []
-    for d in range(n_sta):
-        column = (j + d) % n_sta
+    for d, column in enumerate([j, mate] + [wrap(j + c * CORES, n_sta) for c in range(1, chips)] + [wrap(mate + c * CORES, n_sta) for c in range(1, chips)]):
         edge_copies.append(remote(
-            edge_out.at[0], edge_in.at[1, j], edge_send.at[0, d], edge_recv.at[1, d], ((i + n_src - 1) % n_src, column)))
+            edge_out.at[0], edge_in.at[1, j], edge_send.at[0, d], edge_recv.at[1, j], (wrap(i + n_src - 1, n_src), column)))
         edge_copies.append(remote(
-            edge_out.at[1], edge_in.at[0, j], edge_send.at[1, d], edge_recv.at[0, d], ((i + 1) % n_src, column)))
-
-    pack_copies[0].start()
-    for copy in pack_copies[1:]:
-        copy.start()
+            edge_out.at[1], edge_in.at[0, j], edge_send.at[1, d], edge_recv.at[0, j], (wrap(i + 1, n_src), column)))
+
     for d in range(1, n_sta):
         total_copy(d).start()
+    pack_copies[0].start()
     for copy in lag_copies[1:]:
         copy.start()
 
@@ -111,24 +115,24 @@
     def _():
         lag_group[j, slot] = lag_out[...]
 
-    for copy in edge_copies:
+    for copy in edge_copies[: 2 * CORES] + pack_copies[1:] + edge_copies[2 * CORES :]:
         copy.start()
 
     def send_total(d, carry):
         total_copy(d).start()
         return carry
 
-    lax.fori_loop(n_sta, everyone, send_total, 0)
+    each(n_sta, everyone, send_total)
 
     for d in range(1, n_sta):
         total_copy(d).wait_recv()
     pack_copies[0].wait_recv()
-    for copy in edge_copies:
-        copy.wait_recv()
-    for q in range(per):
-        for c in range(n_sta):
-            landed = remote(
-                lag_out, lag_group.at[c, q], lag_send.at[0], lag_recv.at[q * n_sta + c], (i, mate))
+
+    def take_column(c):
+        for side in range(2):
+            remote(edge_out.at[side], edge_in.at[side, c], edge_send.at[side, 0], edge_recv.at[side, c], (i, mate)).wait_recv()
+        for q in range(per):
+            landed = remote(lag_out, lag_group.at[c, q], lag_send.at[0], lag_recv.at[q * n_sta + c], (i, mate))
 
             @pl.when(jnp.logical_or(j * per + q != i, j != c))
             def _():
@@ -142,6 +146,8 @@
         first = ((chip + phase) % chips) * CORES
         if phase >= 1:
             fwd_copies[phase - 1].wait_recv()
+        for c in range(CORES):
+            take_column(first + c)
         a = packed[first].astype(jnp.float32)
         b = packed[first + 1].astype(jnp.float32)
         wide[pl.ds(offset, half), :] = jnp.where(low_lanes, a, pltpu.roll(b, stations, 1))
@@ -157,14 +163,20 @@
         )
         if phase == 0:
             for c in range(1, chips):
-                pack_copies[c].wait_recv()
-                source = (j + (chips - c) * CORES) % n_sta
+                source = wrap(j + (chips - c) * CORES, n_sta)
                 fwd_copies.append(remote(
                     packed.at[source], packed.at[source], fwd_send.at[c], fwd_recv.at[c], (i, mate)))
-                fwd_copies[-1].start()
 
         def add_lags(coarse, carry):
             start = pl.multiple_of(coarse * SUB, SUB)
+            if phase == 0:
+
+                @pl.when(coarse == LAGS // SUB - 1)
+                def _():
+                    for c in range(1, chips):
+                        pack_copies[c].wait_recv()
+                        fwd_copies[c - 1].start()
+
             for s in range(SUB):
                 lag = (start + s).astype(jnp.float32).astype(jnp.bfloat16)
                 picks[s * 2 * stations : (s + 1) * 2 * stations, :] = jnp.where(
@@ -180,7 +192,7 @@
         total_copy(d).wait_recv()
         return carry
 
-    lax.fori_loop(n_sta, everyone, take_total, 0)
+    each(n_sta, everyone, take_total)
 
     def summed(x):
         return jnp.sum(jnp.sum(jnp.sum(x, axis=0), axis=0), axis=1, keepdims=True)
@@ -200,7 +212,7 @@
         part_copy(d).wait_recv()
         return carry
 
-    lax.fori_loop(1, everyone, send_part, 0)
+    each(1, everyone, send_part)
 
     for copy in edge_copies + pack_copies + fwd_copies + lag_copies[1:]:
         copy.wait_send()
@@ -213,8 +225,8 @@
         total_copy(d).wait_send()
         return carry
 
-    lax.fori_loop(1, everyone, sent, 0)
-    lax.fori_loop(1, everyone, take_part, 0)
+    each(1, everyone, sent)
+    each(1, everyone, take_part)
 
     share = n_src // STEPS
     place = i % per
@@ -231,7 +243,7 @@
         part_copy(d).wait_send()
         return carry
 
-    lax.fori_loop(1, everyone, part_sent, 0)
+    each(1, everyone, part_sent)
 
 
 def on_device(n_src, n_sta, trace, quadrature, gains, lags):
@@ -274,7 +286,7 @@
             dma((everyone,)), dma((everyone,)),
         ],
         compiler_params=pltpu.CompilerParams(
-            collective_id=0, has_side_effects=True, vmem_limit_bytes=48 * 1024 * 1024
+            collective_id=0, has_side_effects=True, vmem_limit_bytes=62 * 1024 * 1024
         ),
     )(trace, quadrature, gains.reshape(1, stations), lags.T)
 

time: 38.8 us -> 34.5 us (0.89)
  local copies, waits for them, and re-layouts: 3.9 us -> 1.24 us
  Pallas kernels: 34.6 us -> 33.1 us
    unnamed x9 -> x1, local copies, waits for them, and re-layouts: 3.9 us -> 1.24 us
    pallas_call x1, Pallas kernels: 34.6 us -> 33.1 us  [on_device(): pl.pallas_call(functools.partial(kernel, n_src, n_sta), out_shape=jax.Sha...]
where the time goes in v3:
time: 34.5 us; the launch traced here: 34.4 us
  Pallas kernels  33.1 us (96%)
  local copies, waits for them, and re-layouts  1.24 us (4%)
    pallas_call x1, Pallas kernels, on_device(): pl.pallas_call(functools.partial(kernel, n_src, n_sta), out_shape=jax.Sha...  33.1 us
    unnamed x1, local copies, waits for them, and re-layouts  1.24 us

profile of v3, /device:TPU:0, one launch (start us, length us, event | category | flops | bytes accessed | tf_op | source)
XLA Modules:
  0.0 34.4 jit_solution(15083933942200305803)
XLA Ops:
  0.0 33.1 %shard_map.46 = f32[2,128]{1,0:T(2,128)} custom-call(f32[64,1032]{1,0:T(8,128)} %trace_hbm.1, f32[64,1032]{1,0:T(8,128)} %quad_hbm.1, f32[1,64]{1,0:T(1,128)} %bitcast.3, s32[64,128]{1,0:T(8,128)} %bitcast.2), custom_call_target="tpu_custom_call" | custom-call | tf_op jit(solution)/shard_map/pallas_call | solution.py:259
  33.1 1.2 %copy.6 = f32[2,128]{1,0:T(2,128)} copy(f32[2,128]{1,0:T(2,128)} %shard_map.46) | data formatting | bytes 2048

commit v4 on v3

--- a/solution.py
+++ b/solution.py
@@ -70,11 +70,11 @@
     lag_out[...] = lags_ref[...].astype(jnp.float32).astype(jnp.bfloat16)
     own_t = (trace_ref[...] * trace_ref[...] + quad_ref[...] * quad_ref[...]).T * gains_ref[...]
     energy_t[LAGS : LAGS + block, :] = own_t
-    edge_out[0] = own_t[:LAGS]
-    edge_out[1] = own_t[block - LAGS :]
     own_total = jnp.sum(own_t, axis=0, keepdims=True)
     total[i, j] = own_total
     own_mean = own_total / block
+    edge_out[0] = (own_t[:LAGS] - own_mean).astype(jnp.bfloat16)
+    edge_out[1] = (own_t[block - LAGS :] - own_mean).astype(jnp.bfloat16)
     offset = LAGS - (LAGS // n_src) * i
     upper = energy_t[pl.ds(offset, half), :] - own_mean
     lower = energy_t[pl.ds(offset + half, half), :] - own_mean
@@ -94,6 +94,10 @@
         remote(lag_out, lag_group.at[j, slot], lag_send.at[d], lag_recv.at[slot * n_sta + j], (wrap(i + d, n_src), owner))
         for d in range(n_src)
     ]
+    beside = (wrap(i + n_src - 1, n_src), wrap(i + 1, n_src))
+    inside = (i > 0, i < n_src - 1)
+    near = list(range(1, 2 * n_sta)) + list(range((n_src - 1) * n_sta, everyone))
+    far = range(2 * n_sta, (n_src - 1) * n_sta)
     edge_copies = []
     for d, column in enumerate([j, mate] + [wrap(j + c * CORES, n_sta) for c in range(1, chips)] + [wrap(mate + c * CORES, n_sta) for c in range(1, chips)]):
         edge_copies.append(remote(
@@ -101,7 +105,7 @@
         edge_copies.append(remote(
             edge_out.at[1], edge_in.at[0, j], edge_send.at[1, d], edge_recv.at[0, j], (wrap(i + 1, n_src), column)))
 
-    for d in range(1, n_sta):
+    for d in near:
         total_copy(d).start()
     pack_copies[0].start()
     for copy in lag_copies[1:]:
@@ -115,22 +119,34 @@
     def _():
         lag_group[j, slot] = lag_out[...]
 
-    for copy in edge_copies[: 2 * CORES] + pack_copies[1:] + edge_copies[2 * CORES :]:
+    def send_edges(low, high):
+        for side in range(2):
+
+            @pl.when(inside[side])
+            def _():
+                for copy in edge_copies[low + side : high : 2]:
+                    copy.start()
+
+    send_edges(0, 2 * CORES)
+    for copy in pack_copies[1:]:
         copy.start()
+    send_edges(2 * CORES, 2 * n_sta)
 
     def send_total(d, carry):
         total_copy(d).start()
         return carry
 
-    each(n_sta, everyone, send_total)
-
-    for d in range(1, n_sta):
+    for d in far:
+        send_total(d, 0)
+
+    for d in near:
         total_copy(d).wait_recv()
     pack_copies[0].wait_recv()
 
     def take_column(c):
         for side in range(2):
-            remote(edge_out.at[side], edge_in.at[side, c], edge_send.at[side, 0], edge_recv.at[side, c], (i, mate)).wait_recv()
+            edge = remote(edge_out.at[side], edge_in.at[side, c], edge_send.at[side, 0], edge_recv.at[side, c], (i, mate))
+            pl.when(inside[side])(edge.wait_recv)
         for q in range(per):
             landed = remote(lag_out, lag_group.at[c, q], lag_send.at[0], lag_recv.at[q * n_sta + c], (i, mate))
 
@@ -154,7 +170,12 @@
         wide[pl.ds(offset + half, half), :] = jnp.where(low_lanes, pltpu.roll(a, stations, 1), b)
         for side, start in ((0, 0), (1, LAGS + block)):
             wide[start : start + LAGS, :] = jnp.concatenate(
-                [edge_in[side, first + c] - total[i, first + c] / block for c in range(CORES)], axis=1
+                [
+                    edge_in[side, first + c].astype(jnp.float32)
+                    + (total[beside[side], first + c] - total[i, first + c]) / block
+                    for c in range(CORES)
+                ],
+                axis=1,
             )
         for s in range(SUB):
             shifted[s] = wide[pl.ds(offset + s, copied), :].astype(jnp.bfloat16)
@@ -192,7 +213,8 @@
         total_copy(d).wait_recv()
         return carry
 
-    each(n_sta, everyone, take_total)
+    for d in far:
+        take_total(d, 0)
 
     def summed(x):
         return jnp.sum(jnp.sum(jnp.sum(x, axis=0), axis=0), axis=1, keepdims=True)
@@ -214,8 +236,14 @@
 
     each(1, everyone, send_part)
 
-    for copy in edge_copies + pack_copies + fwd_copies + lag_copies[1:]:
+    for copy in pack_copies + fwd_copies + lag_copies[1:]:
         copy.wait_send()
+    for side in range(2):
+
+        @pl.when(inside[side])
+        def _():
+            for copy in edge_copies[side::2]:
+                copy.wait_send()
 
     @pl.when(owner != j)
     def _():
@@ -266,8 +294,8 @@
             pltpu.VMEM((stations, block), jnp.float32),
             pltpu.VMEM((stations, cells), jnp.int32),
             pltpu.VMEM((block + 2 * LAGS, stations), jnp.float32),
-            pltpu.VMEM((2, LAGS, stations), jnp.float32),
-            pltpu.VMEM((2, n_sta, LAGS, stations), jnp.float32),
+            pltpu.VMEM((2, LAGS, stations), jnp.bfloat16),
+            pltpu.VMEM((2, n_sta, LAGS, stations), jnp.bfloat16),
             pltpu.VMEM((n_src, n_sta, 1, stations), jnp.float32),
             pltpu.VMEM((stations, cells), jnp.bfloat16),
             pltpu.VMEM((n_sta, per, stations, cells), jnp.bfloat16),

time: 34.5 us -> 32.6 us (0.945)
  Pallas kernels: 33.1 us -> 31.2 us
    pallas_call x1, Pallas kernels: 33.1 us -> 31.2 us  [on_device(): pl.pallas_call(functools.partial(kernel, n_src, n_sta), out_shape=jax.Sha...]
where the time goes in v4:
time: 32.6 us; the launch traced here: 32.4 us
  Pallas kernels  31.2 us (96%)
  local copies, waits for them, and re-layouts  1.24 us (4%)
    pallas_call x1, Pallas kernels, on_device(): pl.pallas_call(functools.partial(kernel, n_src, n_sta), out_shape=jax.Sha...  31.2 us
    unnamed x1, local copies, waits for them, and re-layouts  1.24 us

profile of v4, /device:TPU:0, one launch (start us, length us, event | category | flops | bytes accessed | tf_op | source)
XLA Modules:
  0.0 32.4 jit_solution(4259847191922947099)
XLA Ops:
  0.0 31.2 %shard_map.46 = f32[2,128]{1,0:T(2,128)} custom-call(f32[64,1032]{1,0:T(8,128)} %trace_hbm.1, f32[64,1032]{1,0:T(8,128)} %quad_hbm.1, f32[1,64]{1,0:T(1,128)} %bitcast.3, s32[64,128]{1,0:T(8,128)} %bitcast.2), custom_call_target="tpu_custom_call" | custom-call | tf_op jit(solution)/shard_map/pallas_call | solution.py:287
  31.2 1.2 %copy.6 = f32[2,128]{1,0:T(2,128)} copy(f32[2,128]{1,0:T(2,128)} %shard_map.46) | data formatting | bytes 2048
